TPU v7x, 32 devices: a whole 2x2x4 slice. The times are simulated.
32 devices in a mesh: batch: 2 (over x), row: 16 (over z, y, core).
Axes of the slice: x: 2, y: 2, z: 4, core: 2. Of those that a mesh axis runs over, the one named last changes fastest.
Arguments:
- pred_points: float32 [8, 16384], P(None, ('batch', 'row')), parts along dimension 1, may hold values from 0 to 1
- obs_points: float32 [8, 16384], P(None, ('batch', 'row')), parts along dimension 1, may hold values from 0 to 1
- predicted: float32 [16, 16384], P(None, ('batch', 'row')), parts along dimension 1, may hold values from 0.2 to 5
- observed: float32 [16, 16384], P(None, ('batch', 'row')), parts along dimension 1, may hold values from 0.2 to 5
Outputs:
- log_u: float32 [16, 16384], P(None, ('batch', 'row')), parts along dimension 1
- log_v: float32 [16, 16384], P(None, ('batch', 'row')), parts along dimension 1
There are 2 independent parts, one for each index of `batch`. A program takes and returns all parts, laid end to end along the dimension named above; each array names one. Nothing has to cross between parts.
All inputs are finite; a program needn't handle non-finite values.
Results may differ from a plain program's by a relative error of at most 0.00055.
Values may be sent and summed in bfloat16 or wider, within the bound.
A program may use at most 64 MiB of HBM per device.

v0:
```python
import math

import jax
import jax.numpy as jnp
from jax import lax
from jax.sharding import PartitionSpec as P

ITERS = 3


ENTROPY = 0.1


def kernel_block(source_pts, target_pts):
    squared = jnp.zeros((source_pts.shape[1], target_pts.shape[1]), jnp.float32)
    for coord in range(source_pts.shape[0]):
        gap = source_pts[coord][:, None] - target_pts[coord][None, :]
        squared = squared + gap * gap
    return jnp.exp(-squared / ENTROPY).astype(jnp.bfloat16)


def contract_last(vectors, block):
    return lax.dot_general(
        vectors, block, (((1,), (1,)), ((), ())), preferred_element_type=jnp.float32
    )


def on_device(pred_points, obs_points, predicted, observed):
    local_rows = pred_points.shape[1]
    freq_count = predicted.shape[0]
    obs_all = lax.all_gather(obs_points, "row", axis=1, tiled=True)
    all_points = obs_all.shape[1]
    block_cols = math.gcd(all_points, 2048)
    block_count = all_points // block_cols

    def fresh_rows(first_col, span_cols):
        return kernel_block(pred_points, lax.dynamic_slice_in_dim(obs_all, first_col, span_cols, 1))

    def add_sums(index, running):
        return running + jnp.sum(
            fresh_rows(index * block_cols, block_cols).astype(jnp.float32), axis=1
        )

    row_sums = lax.fori_loop(0, block_count, add_sums, jnp.zeros((local_rows,), jnp.float32))

    def column_step(weights):

        def fill_block(index, partial_value):
            product = jnp.dot(
                weights,
                fresh_rows(index * block_cols, block_cols),
                preferred_element_type=jnp.float32,
            )
            return lax.dynamic_update_slice_in_dim(partial_value, product, index * block_cols, 1)

        partial_value = lax.fori_loop(
            0, block_count, fill_block, jnp.zeros((freq_count, all_points), jnp.float32)
        )
        return lax.psum_scatter(partial_value, "row", scatter_dimension=1, tiled=True)

    scale_u = predicted / row_sums[None, :]
    scale_v = observed
    for iteration in range(ITERS):
        if iteration > 0:
            empty = jnp.zeros((freq_count, local_rows), jnp.float32)
            shard_piece = lax.all_gather(scale_v.astype(jnp.bfloat16), "row", axis=1, tiled=True)
            piece_cols = shard_piece.shape[1]
            sub_width = math.gcd(piece_cols, block_cols)

            def inner_step(index, partial_value):
                offset = index * sub_width
                vectors = lax.dynamic_slice_in_dim(shard_piece, offset, sub_width, 1)
                return partial_value + contract_last(vectors, fresh_rows(offset, sub_width))

            kernel_sums = lax.fori_loop(0, piece_cols // sub_width, inner_step, empty)
            scale_u = predicted / kernel_sums
        scale_v = observed / column_step(scale_u.astype(jnp.bfloat16))
    return (jnp.log(scale_u), jnp.log(scale_v))


def solution(mesh):
    in_specs = (
        P(None, ("batch", "row")),
        P(None, ("batch", "row")),
        P(None, ("batch", "row")),
        P(None, ("batch", "row")),
    )
    out_specs = (P(None, ("batch", "row")), P(None, ("batch", "row")))
    return jax.shard_map(
        on_device, mesh=mesh, in_specs=in_specs, out_specs=out_specs, check_vma=False
    )
```

profile of v0, /device:TPU:0, one launch (start us, length us, event | category | flops | bytes accessed | tf_op | source)
XLA Modules:
  0.0 349.6 jit_solution(3148632044835796659)
XLA Ops:
  7.2 24.1 %all_gather.9 = f32[8,8192]{1,0:T(8,128)S(1)} all-gather(f32[8,512]{1,0:T(8,128)} %param.17), channel_id=1, replica_groups=mesh['batch'=2,'row'=16] {'row'}, dimensions={1}, use_global_device_ids=true | all-gather | bytes 278528 | tf_op jit(solution)/shard_map/all_gather | solution.py:31
  31.3 23.5 %while.84 = (s32[]{:T(128)}, f32[512]{0:T(512)S(1)}, f32[8,512]{1,0:T(8,128)}, f32[8,8192]{1,0:T(8,128)S(1)}, s32[]{:T(128)}, /*index=5*/s32[]{:T(128)}, s32[]{:...) while((s32[]{:T(128)}, f32[512]{0:T(512)S(1)}, f32[8,512]{1,0:T(8,128)}, ...), condition=%wide.region_2.0_spmd.clone, body=%wide.region_0.0_spmd.clone.sunk | while | flops 29360652 | bytes 254265 | solution.py:44
  32.5 4.6 %convert_reduce_fusion.2 = f32[512]{0:T(512)S(1)} fusion(f32[2048]{0:T(1024)S(1)} %bitcast.362, f32[512]{0:T(512)S(1)} %bitcast.404, f32[2048]{0:T(1024)S(1)} %bitcast.356, f32[512]{0:T(512)S(1)} %bitcast.405, f32[2048]{0:T(1024)S(1)} %bitcast.357, f32[512]{0:T(512)S(1)} %bitcast.406, f32[2048]{0:T(1024)S(1)} %bitcast.358, f32[512]{0:T(512)S(1)} %bitcast.407, ...), kind=kLoop, calls=%fused_computation.63.clone.1 | loop fusion | flops 29359616 | bytes 83968 | tf_op jit(solution)/shard_map/while/body/eval_jaxpr/reduce_sum | solution.py:40
  38.4 4.6 %convert_reduce_fusion.2 = f32[512]{0:T(512)S(1)} fusion(f32[2048]{0:T(1024)S(1)} %bitcast.362, f32[512]{0:T(512)S(1)} %bitcast.404, f32[2048]{0:T(1024)S(1)} %bitcast.356, f32[512]{0:T(512)S(1)} %bitcast.405, f32[2048]{0:T(1024)S(1)} %bitcast.357, f32[512]{0:T(512)S(1)} %bitcast.406, f32[2048]{0:T(1024)S(1)} %bitcast.358, f32[512]{0:T(512)S(1)} %bitcast.407, ...), kind=kLoop, calls=%fused_computation.63.clone.1 | loop fusion | flops 29359616 | bytes 83968 | tf_op jit(solution)/shard_map/while/body/eval_jaxpr/reduce_sum | solution.py:40
  44.3 4.6 %convert_reduce_fusion.2 = f32[512]{0:T(512)S(1)} fusion(f32[2048]{0:T(1024)S(1)} %bitcast.362, f32[512]{0:T(512)S(1)} %bitcast.404, f32[2048]{0:T(1024)S(1)} %bitcast.356, f32[512]{0:T(512)S(1)} %bitcast.405, f32[2048]{0:T(1024)S(1)} %bitcast.357, f32[512]{0:T(512)S(1)} %bitcast.406, f32[2048]{0:T(1024)S(1)} %bitcast.358, f32[512]{0:T(512)S(1)} %bitcast.407, ...), kind=kLoop, calls=%fused_computation.63.clone.1 | loop fusion | flops 29359616 | bytes 83968 | tf_op jit(solution)/shard_map/while/body/eval_jaxpr/reduce_sum | solution.py:40
  50.1 4.6 %convert_reduce_fusion.2 = f32[512]{0:T(512)S(1)} fusion(f32[2048]{0:T(1024)S(1)} %bitcast.362, f32[512]{0:T(512)S(1)} %bitcast.404, f32[2048]{0:T(1024)S(1)} %bitcast.356, f32[512]{0:T(512)S(1)} %bitcast.405, f32[2048]{0:T(1024)S(1)} %bitcast.357, f32[512]{0:T(512)S(1)} %bitcast.406, f32[2048]{0:T(1024)S(1)} %bitcast.358, f32[512]{0:T(512)S(1)} %bitcast.407, ...), kind=kLoop, calls=%fused_computation.63.clone.1 | loop fusion | flops 29359616 | bytes 83968 | tf_op jit(solution)/shard_map/while/body/eval_jaxpr/reduce_sum | solution.py:40
  55.5 16.2 %while.81 = (s32[]{:T(128)}, f32[16,8192]{1,0:T(8,128)S(1)}, f32[8,512]{1,0:T(8,128)S(1)}, f32[8,8192]{1,0:T(8,128)S(1)}, bf16[16,512]{1,0:T(8,128)(2,1)S(1)}, /...) while((s32[]{:T(128)}, f32[16,8192]{1,0:T(8,128)S(1)}, ...), condition=%wide.region_4.0_spmd, body=%wide.region_3.0_spmd.sunk | while | flops 60817420 | bytes 393531 | solution.py:56
  72.6 53.2 %reduce-scatter.4.cloned.1.call-done = f32[16,512]{1,0:T(8,128)} async-done(((f32[16,8192]{1,0:T(8,128)}), f32[16,512]{1,0:T(8,128)}) %reduce-scatter.4.cloned.1.call-update) | async-done | bytes 32784 | tf_op jit(solution)/shard_map/reduce_scatter | solution.py:59
  126.5 20.3 %all_gather.10 = bf16[16,8192]{1,0:T(8,128)(2,1)S(1)} all-gather(bf16[16,512]{1,0:T(8,128)(2,1)S(1)} %divide_convert_fusion.2), channel_id=1, replica_groups=mesh['batch'=2,'row'=16] {'row'}, dimensions={1}, use_global_device_ids=true | all-gather | bytes 278528 | tf_op jit(solution)/shard_map/all_gather | solution.py:66
  146.9 16.3 %while.85 = (s32[]{:T(128)}, f32[16,512]{1,0:T(8,128)S(1)}, bf16[16,8192]{1,0:T(8,128)(2,1)S(1)}, f32[8,512]{1,0:T(8,128)S(1)}, f32[8,8192]{1,0:T(8,128)S(1)}, /...) while((s32[]{:T(128)}, f32[16,512]{1,0:T(8,128)S(1)}, ...), condition=%wide.region_7.0_spmd.clone, body=%wide.region_6.0_spmd.clone.sunk | while | flops 60833804 | bytes 377157 | solution.py:75
  147.1 3.8 %fusion.101 = f32[16,512]{1,0:T(8,128)S(1)} fusion(f32[2048]{0:T(1024)S(1)} %bitcast.322, f32[512]{0:T(512)S(1)} %bitcast.364, f32[2048]{0:T(1024)S(1)} %bitcast.316, f32[512]{0:T(512)S(1)} %bitcast.365, f32[2048]{0:T(1024)S(1)} %bitcast.317, f32[512]{0:T(512)S(1)} %bitcast.366, f32[2048]{0:T(1024)S(1)} %bitcast.318, f32[512]{0:T(512)S(1)} %bitcast.367, ...), kind=kOutput, calls=%fused_computation.69.clone.1 | convolution fusion | flops 60833792 | bytes 212997 | tf_op jit(solution)/shard_map/while/body/eval_jaxpr/dot_general | solution.py:23
  151.1 3.8 %fusion.101 = f32[16,512]{1,0:T(8,128)S(1)} fusion(f32[2048]{0:T(1024)S(1)} %bitcast.322, f32[512]{0:T(512)S(1)} %bitcast.364, f32[2048]{0:T(1024)S(1)} %bitcast.316, f32[512]{0:T(512)S(1)} %bitcast.365, f32[2048]{0:T(1024)S(1)} %bitcast.317, f32[512]{0:T(512)S(1)} %bitcast.366, f32[2048]{0:T(1024)S(1)} %bitcast.318, f32[512]{0:T(512)S(1)} %bitcast.367, ...), kind=kOutput, calls=%fused_computation.69.clone.1 | convolution fusion | flops 60833792 | bytes 212997 | tf_op jit(solution)/shard_map/while/body/eval_jaxpr/dot_general | solution.py:23
  155.2 3.8 %fusion.101 = f32[16,512]{1,0:T(8,128)S(1)} fusion(f32[2048]{0:T(1024)S(1)} %bitcast.322, f32[512]{0:T(512)S(1)} %bitcast.364, f32[2048]{0:T(1024)S(1)} %bitcast.316, f32[512]{0:T(512)S(1)} %bitcast.365, f32[2048]{0:T(1024)S(1)} %bitcast.317, f32[512]{0:T(512)S(1)} %bitcast.366, f32[2048]{0:T(1024)S(1)} %bitcast.318, f32[512]{0:T(512)S(1)} %bitcast.367, ...), kind=kOutput, calls=%fused_computation.69.clone.1 | convolution fusion | flops 60833792 | bytes 212997 | tf_op jit(solution)/shard_map/while/body/eval_jaxpr/dot_general | solution.py:23
  159.3 3.8 %fusion.101 = f32[16,512]{1,0:T(8,128)S(1)} fusion(f32[2048]{0:T(1024)S(1)} %bitcast.322, f32[512]{0:T(512)S(1)} %bitcast.364, f32[2048]{0:T(1024)S(1)} %bitcast.316, f32[512]{0:T(512)S(1)} %bitcast.365, f32[2048]{0:T(1024)S(1)} %bitcast.317, f32[512]{0:T(512)S(1)} %bitcast.366, f32[2048]{0:T(1024)S(1)} %bitcast.318, f32[512]{0:T(512)S(1)} %bitcast.367, ...), kind=kOutput, calls=%fused_computation.69.clone.1 | convolution fusion | flops 60833792 | bytes 212997 | tf_op jit(solution)/shard_map/while/body/eval_jaxpr/dot_general | solution.py:23
  163.2 16.2 %while.82 = (s32[]{:T(128)}, f32[16,8192]{1,0:T(8,128)S(1)}, f32[8,512]{1,0:T(8,128)S(1)}, f32[8,8192]{1,0:T(8,128)S(1)}, bf16[16,512]{1,0:T(8,128)(2,1)S(1)}, /...) while((s32[]{:T(128)}, f32[16,8192]{1,0:T(8,128)S(1)}, ...), condition=%wide.region_9.0_spmd, body=%wide.region_8.0_spmd.sunk | while | flops 60817420 | bytes 393531 | solution.py:56
  180.3 53.1 %reduce-scatter.6.cloned.1.call-done = f32[16,512]{1,0:T(8,128)} async-done(((f32[16,8192]{1,0:T(8,128)}), f32[16,512]{1,0:T(8,128)}) %reduce-scatter.6.cloned.1.call-update) | async-done | bytes 32784 | tf_op jit(solution)/shard_map/reduce_scatter | solution.py:59
  234.1 20.4 %all_gather.11 = bf16[16,8192]{1,0:T(8,128)(2,1)S(1)} all-gather(bf16[16,512]{1,0:T(8,128)(2,1)S(1)} %divide_convert_fusion), channel_id=1, replica_groups=mesh['batch'=2,'row'=16] {'row'}, dimensions={1}, use_global_device_ids=true | all-gather | bytes 278528 | tf_op jit(solution)/shard_map/all_gather | solution.py:66
  254.5 16.3 %while.86 = (s32[]{:T(128)}, f32[16,512]{1,0:T(8,128)S(1)}, bf16[16,8192]{1,0:T(8,128)(2,1)S(1)}, f32[8,512]{1,0:T(8,128)S(1)}, f32[8,8192]{1,0:T(8,128)S(1)}, /...) while((s32[]{:T(128)}, f32[16,512]{1,0:T(8,128)S(1)}, ...), condition=%wide.region_12.0_spmd.clone, body=%wide.region_11.0_spmd.clone.sunk | while | flops 60833804 | bytes 377157 | solution.py:75
  254.8 3.8 %fusion.104 = f32[16,512]{1,0:T(8,128)S(1)} fusion(f32[2048]{0:T(1024)S(1)} %bitcast.330, f32[512]{0:T(512)S(1)} %bitcast.372, f32[2048]{0:T(1024)S(1)} %bitcast.324, f32[512]{0:T(512)S(1)} %bitcast.373, f32[2048]{0:T(1024)S(1)} %bitcast.325, f32[512]{0:T(512)S(1)} %bitcast.374, f32[2048]{0:T(1024)S(1)} %bitcast.326, f32[512]{0:T(512)S(1)} %bitcast.375, ...), kind=kOutput, calls=%fused_computation.76.clone.1 | convolution fusion | flops 60833792 | bytes 212997 | tf_op jit(solution)/shard_map/while/body/eval_jaxpr/dot_general | solution.py:23
  258.8 3.8 %fusion.104 = f32[16,512]{1,0:T(8,128)S(1)} fusion(f32[2048]{0:T(1024)S(1)} %bitcast.330, f32[512]{0:T(512)S(1)} %bitcast.372, f32[2048]{0:T(1024)S(1)} %bitcast.324, f32[512]{0:T(512)S(1)} %bitcast.373, f32[2048]{0:T(1024)S(1)} %bitcast.325, f32[512]{0:T(512)S(1)} %bitcast.374, f32[2048]{0:T(1024)S(1)} %bitcast.326, f32[512]{0:T(512)S(1)} %bitcast.375, ...), kind=kOutput, calls=%fused_computation.76.clone.1 | convolution fusion | flops 60833792 | bytes 212997 | tf_op jit(solution)/shard_map/while/body/eval_jaxpr/dot_general | solution.py:23
  262.9 3.8 %fusion.104 = f32[16,512]{1,0:T(8,128)S(1)} fusion(f32[2048]{0:T(1024)S(1)} %bitcast.330, f32[512]{0:T(512)S(1)} %bitcast.372, f32[2048]{0:T(1024)S(1)} %bitcast.324, f32[512]{0:T(512)S(1)} %bitcast.373, f32[2048]{0:T(1024)S(1)} %bitcast.325, f32[512]{0:T(512)S(1)} %bitcast.374, f32[2048]{0:T(1024)S(1)} %bitcast.326, f32[512]{0:T(512)S(1)} %bitcast.375, ...), kind=kOutput, calls=%fused_computation.76.clone.1 | convolution fusion | flops 60833792 | bytes 212997 | tf_op jit(solution)/shard_map/while/body/eval_jaxpr/dot_general | solution.py:23
  267.0 3.8 %fusion.104 = f32[16,512]{1,0:T(8,128)S(1)} fusion(f32[2048]{0:T(1024)S(1)} %bitcast.330, f32[512]{0:T(512)S(1)} %bitcast.372, f32[2048]{0:T(1024)S(1)} %bitcast.324, f32[512]{0:T(512)S(1)} %bitcast.373, f32[2048]{0:T(1024)S(1)} %bitcast.325, f32[512]{0:T(512)S(1)} %bitcast.374, f32[2048]{0:T(1024)S(1)} %bitcast.326, f32[512]{0:T(512)S(1)} %bitcast.375, ...), kind=kOutput, calls=%fused_computation.76.clone.1 | convolution fusion | flops 60833792 | bytes 212997 | tf_op jit(solution)/shard_map/while/body/eval_jaxpr/dot_general | solution.py:23
  271.5 16.2 %while.83 = (s32[]{:T(128)}, f32[16,8192]{1,0:T(8,128)S(1)}, f32[8,512]{1,0:T(8,128)S(1)}, f32[8,8192]{1,0:T(8,128)S(1)}, bf16[16,512]{1,0:T(8,128)(2,1)S(1)}, /...) while((s32[]{:T(128)}, f32[16,8192]{1,0:T(8,128)S(1)}, ...), condition=%wide.region_14.0_spmd, body=%wide.region_13.0_spmd.sunk | while | flops 60817420 | bytes 393531 | solution.py:56
  288.5 53.2 %reduce-scatter.8.cloned.1.call-done = f32[16,512]{1,0:T(8,128)} async-done(((f32[16,8192]{1,0:T(8,128)}), f32[16,512]{1,0:T(8,128)}) %reduce-scatter.8.cloned.1.call-update) | async-done | bytes 32784 | tf_op jit(solution)/shard_map/reduce_scatter | solution.py:59
  (94 shorter events, 62.0 us)
Async XLA Ops:
  7.2 118.6 %reduce-scatter.4.cloned.1.call-start = ((), (), s32[]{:S(2)}) async-start(), calls=%async_computation.3 | async-start | bytes 557056 | tf_op jit(solution)/shard_map/reduce_scatter | solution.py:59
  31.3 23.5 %copy-start.4 = (f32[16,512]{1,0:T(8,128)S(1)}, f32[16,512]{1,0:T(8,128)}, u32[]{:S(2)}) copy-start(f32[16,512]{1,0:T(8,128)} %param.18) | copy-start | bytes 98308
  54.8 0.7 copy-start
  71.7 0.8 copy-start.2
  71.7 54.1 %copy-start.5 = (f32[16,512]{1,0:T(8,128)S(1)}, f32[16,512]{1,0:T(8,128)}, u32[]{:S(2)}) copy-start(f32[16,512]{1,0:T(8,128)} %param.19) | copy-start | bytes 98308
  72.5 160.9 %reduce-scatter.6.cloned.1.call-start = ((), (), s32[]{:S(2)}) async-start(), calls=%async_computation.4 | async-start | bytes 557056 | tf_op jit(solution)/shard_map/reduce_scatter | solution.py:59
  179.4 0.8 copy-start.3
  180.2 161.5 %reduce-scatter.8.cloned.1.call-start = ((), (), s32[]{:S(2)}) async-start(), calls=%async_computation.5 | async-start | bytes 557056 | tf_op jit(solution)/shard_map/reduce_scatter | solution.py:59
  287.7 0.8 copy-start.1
Sparse Core Ops, SparseCore 0:
  72.6 53.0 reduce-scatter.3
  180.3 52.9 reduce-scatter.5
  288.6 53.0 reduce-scatter.7
where the time goes:
time: 350 us
  waiting for transfers between devices  159 us (45%)
  matrix products  76.5 us (22%)
  blocking collectives  64.8 us (19%)
  other arithmetic  22.1 us (6%)
  between operations  13.8 us (4%)
  local copies, waits for them, and re-layouts  12.3 us (4%)
    reduce_scatter x3, waiting for transfers between devices, column_step(): lax.psum_scatter(partial_value, 'row', scatter_dimension=1, tiled=True)  159 us
    dot_general x12, matrix products, fill_block(): jnp.dot(weights, fresh_rows(index * block_cols, block_cols), preferred_el...  45.8 us
    all_gather x2, blocking collectives, on_device(): lax.all_gather(scale_v.astype(jnp.bfloat16), 'row', axis=1, tiled=True)  40.7 us
    dot_general x8, matrix products, contract_last(): lax.dot_general(vectors, block, (((1,), (1,)), ((), ())), preferred_eleme...  30.7 us
    all_gather x1, blocking collectives, on_device(): obs_all = lax.all_gather(obs_points, 'row', axis=1, tiled=True)  24.1 us
    reduce_sum x4, other arithmetic, add_sums(): jnp.sum(fresh_rows(index * block_cols, block_cols).astype(jnp.float32), a...  18.4 us
    slice x48, local copies, waits for them, and re-layouts, kernel_block(): gap = source_pts[coord][:, None] - target_pts[coord][None, :]  9.13 us
  transfers between devices with their start and end apart: 3, of which 3 were waited for; matrix products, arithmetic and copies ran while one was open for 0% of the time, Pallas kernels for 0%

commit v1 on v0

v1 whole, which is shorter than its diff:
```python
import functools

import jax
import jax.numpy as jnp
from jax import lax
from jax.experimental import pallas as pl
from jax.experimental.pallas import tpu as pltpu
from jax.sharding import PartitionSpec as P

ITERS = 3
ENTROPY = 0.1
DEPTH = 64


def xor_index(left, right, bits):
    total = 0
    for bit in range(bits):
        unit = 1 << bit
        total = total + unit * ((left // unit + right // unit) % 2)
    return total


def three_parts(value):
    first = value.astype(jnp.bfloat16).astype(jnp.float32)
    rest = value - first
    second = rest.astype(jnp.bfloat16).astype(jnp.float32)
    return first, second, rest - second


def operand(points, is_source):
    centred = points - 0.5
    norm = jnp.sum(centred * centred, axis=0, keepdims=True) * (-1.0 / ENTROPY)
    n1, n2, n3 = three_parts(jnp.broadcast_to(norm, points.shape))
    row = lax.broadcasted_iota(jnp.int32, points.shape, 0)
    one, zero = jnp.ones_like(points), jnp.zeros_like(points)
    if is_source:
        a1, a2, a3 = three_parts(centred * (2.0 / ENTROPY))
        pieces = [a1, a1, a2, a2, a1, a3]
        n_first, one_first = 0, 3
    else:
        b1, b2, b3 = three_parts(centred)
        pieces = [b1, b2, b1, b2, b3, b1]
        n_first, one_first = 3, 0
    norms = jnp.where((row >= one_first) & (row < one_first + 3), one, zero)
    for place, part in enumerate((n1, n2, n3)):
        norms = jnp.where(row == n_first + place, part, norms)
    return jnp.concatenate(pieces + [norms, zero], axis=0)


def kernel(
    chips, pred_ref, obs_ref, predicted_ref, observed_ref, u_ref, v_ref,
    obs_buf, pred_buf, predicted_buf, source, cells, acc, weights,
    col_send, col_recv, v_send, v_recv, row_send, row_recv,
    obs_sems, col_sems, v_sems, sib_sems,
):
    points = pred_ref.shape[1]
    freqs = predicted_ref.shape[0]
    me = lax.axis_index("row")
    core, chip = me % 2, me // 2
    sibling = {"row": me + 1 - 2 * core}
    bits = chips.bit_length() - 1
    power = chips == 1 << bits

    def ahead(step):
        other = xor_index(chip, step, bits) if power else (chip + step) % chips
        return {"row": other * 2 + core}

    def behind(step):
        other = xor_index(chip, step, bits) if power else (chip + chips - step) % chips
        return {"row": other * 2 + core}

    def remote(src, dst, sems, place, target):
        return pltpu.make_async_remote_copy(
            src_ref=src, dst_ref=dst, send_sem=sems.at[(0, *place)], recv_sem=sems.at[(1, *place)],
            device_id=target, device_id_type=pl.DeviceIdType.MESH,
        )

    def obs_copy(step):
        return remote(obs_ref, obs_buf.at[step], obs_sems, (step,), ahead(step))

    def col_copy(k, step):
        return remote(col_send.at[k, step], col_recv.at[k, step], col_sems, (k, step), behind(step))

    def v_copy(k, step):
        return remote(v_send.at[k], v_recv.at[k, step], v_sems, (k, step), ahead(step))

    def row_copy(k):
        return remote(row_send.at[k], row_recv.at[k], sib_sems, (2 + k,), sibling)

    pred_copy = remote(pred_ref, pred_buf, sib_sems, (0,), sibling)
    predicted_copy = remote(predicted_ref, predicted_buf, sib_sems, (1,), sibling)

    def each(first, last, act):
        lax.fori_loop(first, last, lambda at, _: (act(at), 0)[1], 0)

    barrier = pltpu.get_barrier_semaphore()
    pl.semaphore_signal(barrier, inc=1, device_id=sibling, device_id_type=pl.DeviceIdType.MESH)
    each(1, chips, lambda step: pl.semaphore_signal(
        barrier, inc=1, device_id=ahead(step), device_id_type=pl.DeviceIdType.MESH))
    obs_buf[0] = obs_ref[...]
    acc[...] = jnp.zeros_like(acc)
    source[:points] = operand(pred_ref[...], True).T.astype(jnp.bfloat16)
    pl.semaphore_wait(barrier, chips)

    pred_copy.start()
    each(1, chips, lambda at: obs_copy(chips - at).start())
    predicted_copy.start()
    pred_copy.wait_recv()
    source[points:] = operand(pred_buf[...], True).T.astype(jnp.bfloat16)

    tile = min(256, points)

    def build(step):
        @pl.when(step > 0)
        def _():
            obs_copy(step).wait_recv()

        target = operand(obs_buf[step], False).astype(jnp.bfloat16)
        for first in range(0, 2 * points, tile):
            rows = slice(first, first + tile)
            exponent = jnp.dot(source[rows], target, preferred_element_type=jnp.float32)
            block = jnp.exp(exponent).astype(jnp.bfloat16)
            cells[step, rows] = block
            wide = block.astype(jnp.float32)
            sums = acc[rows]
            for lane in range(0, points, 128):
                sums = sums + wide[:, lane:lane + 128]
            acc[rows] = sums

    each(0, chips, build)
    row_sums = jnp.sum(acc[...].T, axis=0, keepdims=True)
    row_send[0] = jnp.broadcast_to(row_sums, row_send.shape[1:])
    row_copy(0).start()
    predicted_copy.wait_recv()

    for k in range(ITERS):
        if k > 0:
            @pl.when(chips > 1)
            def _():
                each(1, chips, lambda at: v_copy(k - 1, chips - at).start())

            def add_rows(step, total):
                @pl.when(step > 0)
                def _():
                    v_copy(k - 1, step).wait_recv()

                return total + lax.dot_general(
                    v_recv[k - 1, step], cells[step], (((1,), (1,)), ((), ())),
                    preferred_element_type=jnp.float32,
                )

            row_send[k] = lax.fori_loop(
                0, chips, add_rows, jnp.zeros((freqs, 2 * points), jnp.float32))
            row_copy(k).start()
        row_copy(k).wait_recv()
        own = predicted_ref[...] / (row_send[k, :, :points] + row_recv[k, :, points:])
        other = predicted_buf[...] / (row_send[k, :, points:] + row_recv[k, :, :points])
        weights[:, :points] = own.astype(jnp.bfloat16)
        weights[:, points:] = other.astype(jnp.bfloat16)
        if k == ITERS - 1:
            u_ref[...] = own

        def columns(at):
            step = chips - at
            col_send[k, step] = jnp.dot(
                weights[...], cells[step], preferred_element_type=jnp.float32
            )
            col_copy(k, step).start()

        each(1, chips, columns)
        total = jnp.dot(weights[...], cells[0], preferred_element_type=jnp.float32)

        def add_columns(step, total):
            col_copy(k, step).wait_recv()
            return total + col_recv[k, step].astype(jnp.float32)

        total = lax.fori_loop(1, chips, add_columns, total)
        scale_v = observed_ref[...] / total
        if k < ITERS - 1:
            v_send[k] = scale_v.astype(jnp.bfloat16)
            v_recv[k, 0] = scale_v.astype(jnp.bfloat16)
        else:
            v_ref[...] = scale_v

    pred_copy.wait_send()
    predicted_copy.wait_send()
    for k in range(ITERS):
        row_copy(k).wait_send()

    def drain(step):
        obs_copy(step).wait_send()
        for k in range(ITERS):
            col_copy(k, step).wait_send()
        for k in range(ITERS - 1):
            v_copy(k, step).wait_send()

    each(1, chips, drain)


def on_device(chips, pred_points, obs_points, predicted, observed):
    coords, points = pred_points.shape
    freqs = predicted.shape[0]
    f32, bf16 = jnp.float32, jnp.bfloat16
    vmem = pl.BlockSpec(memory_space=pltpu.VMEM)
    cell_bytes = chips * 2 * points * points * 2
    pairs = chips * 2 * points * points
    scale_u, scale_v = pl.pallas_call(
        functools.partial(kernel, chips),
        out_shape=[jax.ShapeDtypeStruct((freqs, points), f32)] * 2,
        in_specs=[vmem] * 4,
        out_specs=[vmem] * 2,
        scratch_shapes=[
            pltpu.VMEM((chips, coords, points), f32),
            pltpu.VMEM((coords, points), f32),
            pltpu.VMEM((freqs, points), f32),
            pltpu.VMEM((2 * points, DEPTH), bf16),
            pltpu.VMEM((chips, 2 * points, points), bf16),
            pltpu.VMEM((2 * points, 128), f32),
            pltpu.VMEM((freqs, 2 * points), bf16),
            pltpu.VMEM((ITERS, chips, freqs, points), f32),
            pltpu.VMEM((ITERS, chips, freqs, points), f32),
            pltpu.VMEM((ITERS - 1, freqs, points), bf16),
            pltpu.VMEM((ITERS - 1, chips, freqs, points), bf16),
            pltpu.VMEM((ITERS, freqs, 2 * points), f32),
            pltpu.VMEM((ITERS, freqs, 2 * points), f32),
            pltpu.SemaphoreType.DMA((2, chips)),
            pltpu.SemaphoreType.DMA((2, ITERS, chips)),
            pltpu.SemaphoreType.DMA((2, ITERS - 1, chips)),
            pltpu.SemaphoreType.DMA((2, 2 + ITERS)),
        ],
        compiler_params=pltpu.CompilerParams(
            collective_id=0, has_side_effects=True,
            vmem_limit_bytes=cell_bytes + 24 * 2**20,
        ),
        cost_estimate=pl.CostEstimate(
            flops=pairs * (2 * DEPTH + 5 * 2 * freqs),
            bytes_accessed=4 * points * (2 * coords + 4 * freqs),
            transcendentals=pairs,
        ),
    )(pred_points, obs_points, predicted, observed)
    return jnp.log(scale_u), jnp.log(scale_v)


def solution(mesh):
    spec = P(None, ("batch", "row"))
    return jax.shard_map(
        functools.partial(on_device, mesh.shape["row"] // 2), mesh=mesh,
        in_specs=(spec,) * 4, out_specs=(spec,) * 2, check_vma=False,
    )
```

time: 350 us -> 57.4 us (0.16)
  waiting for transfers between devices: 159 us -> 0 us
  matrix products: 76.5 us -> 0 us
  blocking collectives: 64.8 us -> 0 us
  Pallas kernels: 0 us -> 52.2 us
  other arithmetic: 22.1 us -> 0 us
  between operations: 13.8 us -> 0.65 us
  local copies, waits for them, and re-layouts: 12.3 us -> 4.19 us
    reduce_scatter x3 -> x0, waiting for transfers between devices: 159 us -> none  [column_step(): lax.psum_scatter(partial_value, 'row', scatter_dimension=1, tiled=True)]
    dot_general x20 -> x0, matrix products: 76.5 us -> none  [the longest x12 45.8 us: fill_block(): jnp.dot(weights, fresh_rows(index * block_cols, block_cols), preferred_el...]
    all_gather x3 -> x0, blocking collectives: 64.8 us -> none  [the longest x2 40.7 us: on_device(): lax.all_gather(scale_v.astype(jnp.bfloat16), 'row', axis=1, tiled=True)]
    pallas_call x0 -> x1, Pallas kernels: none -> 52.2 us  [on_device(): pl.pallas_call(functools.partial(kernel, chips), out_shape=[jax.ShapeDtyp...]
    reduce_sum x4 -> x0, other arithmetic: 18.4 us -> none  [add_sums(): jnp.sum(fresh_rows(index * block_cols, block_cols).astype(jnp.float32), a...]
    slice x48 -> x0, local copies, waits for them, and re-layouts: 9.13 us -> none  [kernel_block(): gap = source_pts[coord][:, None] - target_pts[coord][None, :]]
  transfers between devices with their start and end apart: 3 -> 0, of which waited for: 3 -> 0; matrix products, arithmetic and copies ran while one was open for 0% -> 0% of each run, Pallas kernels for 0% -> 0%
where the time goes in v1:
time: 57.4 us; the launch traced here: 57 us
  Pallas kernels  52.2 us (91%)
  local copies, waits for them, and re-layouts  4.19 us (7%)
  between operations  0.65 us (1%)
    pallas_call x1, Pallas kernels, on_device(): pl.pallas_call(functools.partial(kernel, chips), out_shape=[jax.ShapeDtyp...  52.2 us
    unnamed x8, local copies, waits for them, and re-layouts  2.94 us
    log x2, local copies, waits for them, and re-layouts, on_device(): return (jnp.log(scale_u), jnp.log(scale_v))  1.25 us

profile of v1, /device:TPU:0, one launch (start us, length us, event | category | flops | bytes accessed | tf_op | source)
XLA Modules:
  0.0 57.0 jit_solution(38320117188962559)
XLA Ops:
  0.6 0.0 copy-start
  0.6 0.7 %copy-done = f32[16,512]{1,0:T(8,128)S(1)} copy-done((f32[16,512]{1,0:T(8,128)S(1)}, f32[16,512]{1,0:T(8,128)}, u32[]{:S(2)}) %copy-start) | copy-done | bytes 32792
  1.4 0.0 copy-start.1
  1.4 0.8 %copy-done.1 = f32[16,512]{1,0:T(8,128)S(1)} copy-done((f32[16,512]{1,0:T(8,128)S(1)}, f32[16,512]{1,0:T(8,128)}, u32[]{:S(2)}) %copy-start.1) | copy-done | bytes 32792
  2.1 0.0 copy-start.2
  2.1 0.7 %copy-done.2 = f32[8,512]{1,0:T(8,128)S(1)} copy-done((f32[8,512]{1,0:T(8,128)S(1)}, f32[8,512]{1,0:T(8,128)}, u32[]{:S(2)}) %copy-start.2) | copy-done | bytes 16408
  2.9 0.0 copy-start.3
  2.9 0.7 %copy-done.3 = f32[8,512]{1,0:T(8,128)S(1)} copy-done((f32[8,512]{1,0:T(8,128)S(1)}, f32[8,512]{1,0:T(8,128)}, u32[]{:S(2)}) %copy-start.3) | copy-done | bytes 16408
  3.6 52.2 %shard_map.59 = (f32[16,512]{1,0:T(8,128)S(1)}, f32[16,512]{1,0:T(8,128)S(1)}) custom-call(f32[8,512]{1,0:T(8,128)S(1)} %copy-done.2, f32[8,512]{1,0:T(8,128)S(1)} %copy-done.3, f32[16,512]{1,0:T(8,128)S(1)} %copy-done, f32[16,512]{1,0:T(8,128)S(1)} %copy-done.1), custom_call_target="tpu_custom_call" | custom-call | flops 1207959552 | bytes 163840 | tf_op jit(solution)/shard_map/pallas_call | solution.py:207
  55.8 0.6 %log.6 = f32[16,512]{1,0:T(8,128)} log(f32[16,512]{1,0:T(8,128)S(1)} %get-tuple-element.4) | non-fusion elementwise | bytes 65536 | tf_op jit(solution)/shard_map/log | solution.py:241
  56.4 0.6 %log.7 = f32[16,512]{1,0:T(8,128)} log(f32[16,512]{1,0:T(8,128)S(1)} %get-tuple-element.5) | non-fusion elementwise | bytes 65536 | tf_op jit(solution)/shard_map/log | solution.py:241
Async XLA Ops:
  0.6 0.8 %copy-start = (f32[16,512]{1,0:T(8,128)S(1)}, f32[16,512]{1,0:T(8,128)}, u32[]{:S(2)}) copy-start(f32[16,512]{1,0:T(8,128)} %predicted_ref.1) | copy-start | bytes 98308
  1.4 0.8 %copy-start.1 = (f32[16,512]{1,0:T(8,128)S(1)}, f32[16,512]{1,0:T(8,128)}, u32[]{:S(2)}) copy-start(f32[16,512]{1,0:T(8,128)} %observed_ref.1) | copy-start | bytes 98308
  2.1 0.7 %copy-start.2 = (f32[8,512]{1,0:T(8,128)S(1)}, f32[8,512]{1,0:T(8,128)}, u32[]{:S(2)}) copy-start(f32[8,512]{1,0:T(8,128)} %pred_ref.1) | copy-start | bytes 49156
  2.9 0.7 %copy-start.3 = (f32[8,512]{1,0:T(8,128)S(1)}, f32[8,512]{1,0:T(8,128)}, u32[]{:S(2)}) copy-start(f32[8,512]{1,0:T(8,128)} %obs_ref.1) | copy-start | bytes 49156

commit v2 on v1

--- a/solution.py
+++ b/solution.py
@@ -48,10 +48,12 @@
 
 
 def kernel(
-    chips, pred_ref, obs_ref, predicted_ref, observed_ref, u_ref, v_ref,
+    chips, pred_in, obs_in, predicted_in, observed_in, scale_ref,
+    pred_ref, predicted_ref, observed_ref,
     obs_buf, pred_buf, predicted_buf, source, cells, acc, weights,
-    col_send, col_recv, v_send, v_recv, row_send, row_recv,
-    obs_sems, col_sems, v_sems, sib_sems,
+    first_send, first_recv, col_send, col_recv, known,
+    v_send, v_recv, row_send, row_recv,
+    in_sems, obs_sems, col_sems, v_sems, sib_sems,
 ):
     points = pred_ref.shape[1]
     freqs = predicted_ref.shape[0]
@@ -76,10 +78,13 @@
         )
 
     def obs_copy(step):
-        return remote(obs_ref, obs_buf.at[step], obs_sems, (step,), ahead(step))
+        return remote(obs_buf.at[0], obs_buf.at[step], obs_sems, (step,), ahead(step))
 
     def col_copy(k, step):
-        return remote(col_send.at[k, step], col_recv.at[k, step], col_sems, (k, step), behind(step))
+        if k == 0:
+            return remote(first_send.at[step], first_recv.at[step], col_sems, (k, step), behind(step))
+        return remote(
+            col_send.at[k - 1, step], col_recv.at[k - 1, step], col_sems, (k, step), behind(step))
 
     def v_copy(k, step):
         return remote(v_send.at[k], v_recv.at[k, step], v_sems, (k, step), ahead(step))
@@ -93,30 +98,24 @@
     def each(first, last, act):
         lax.fori_loop(first, last, lambda at, _: (act(at), 0)[1], 0)
 
+    fetches = [
+        pltpu.make_async_copy(src, dst, in_sems.at[place])
+        for place, (src, dst) in enumerate((
+            (pred_in, pred_ref), (obs_in, obs_buf.at[0]),
+            (predicted_in, predicted_ref), (observed_in, observed_ref),
+        ))
+    ]
+    for fetch in fetches:
+        fetch.start()
     barrier = pltpu.get_barrier_semaphore()
     pl.semaphore_signal(barrier, inc=1, device_id=sibling, device_id_type=pl.DeviceIdType.MESH)
     each(1, chips, lambda step: pl.semaphore_signal(
         barrier, inc=1, device_id=ahead(step), device_id_type=pl.DeviceIdType.MESH))
-    obs_buf[0] = obs_ref[...]
     acc[...] = jnp.zeros_like(acc)
-    source[:points] = operand(pred_ref[...], True).T.astype(jnp.bfloat16)
-    pl.semaphore_wait(barrier, chips)
-
-    pred_copy.start()
-    each(1, chips, lambda at: obs_copy(chips - at).start())
-    predicted_copy.start()
-    pred_copy.wait_recv()
-    source[points:] = operand(pred_buf[...], True).T.astype(jnp.bfloat16)
-
     tile = min(256, points)
 
-    def build(step):
-        @pl.when(step > 0)
-        def _():
-            obs_copy(step).wait_recv()
-
-        target = operand(obs_buf[step], False).astype(jnp.bfloat16)
-        for first in range(0, 2 * points, tile):
+    def build(step, target, first_row, last_row):
+        for first in range(first_row, last_row, tile):
             rows = slice(first, first + tile)
             exponent = jnp.dot(source[rows], target, preferred_element_type=jnp.float32)
             block = jnp.exp(exponent).astype(jnp.bfloat16)
@@ -127,17 +126,36 @@
                 sums = sums + wide[:, lane:lane + 128]
             acc[rows] = sums
 
-    each(0, chips, build)
+    fetches[0].wait()
+    source[:points] = operand(pred_ref[...], True).T.astype(jnp.bfloat16)
+    fetches[1].wait()
+    own_target = operand(obs_buf[0], False).astype(jnp.bfloat16)
+    build(0, own_target, 0, points)
+    pl.semaphore_wait(barrier, chips)
+
+    pred_copy.start()
+    each(1, chips, lambda at: obs_copy(chips - at).start())
+    fetches[2].wait()
+    predicted_copy.start()
+    fetches[3].wait()
+    pred_copy.wait_recv()
+    source[points:] = operand(pred_buf[...], True).T.astype(jnp.bfloat16)
+    build(0, own_target, points, 2 * points)
+
+    def build_next(step):
+        obs_copy(step).wait_recv()
+        build(step, operand(obs_buf[step], False).astype(jnp.bfloat16), 0, 2 * points)
+
+    each(1, chips, build_next)
     row_sums = jnp.sum(acc[...].T, axis=0, keepdims=True)
     row_send[0] = jnp.broadcast_to(row_sums, row_send.shape[1:])
     row_copy(0).start()
     predicted_copy.wait_recv()
 
+    others = jnp.zeros((freqs, points), jnp.float32)
     for k in range(ITERS):
         if k > 0:
-            @pl.when(chips > 1)
-            def _():
-                each(1, chips, lambda at: v_copy(k - 1, chips - at).start())
+            each(1, chips, lambda at: v_copy(k - 1, chips - at).start())
 
             def add_rows(step, total):
                 @pl.when(step > 0)
@@ -158,29 +176,37 @@
         weights[:, :points] = own.astype(jnp.bfloat16)
         weights[:, points:] = other.astype(jnp.bfloat16)
         if k == ITERS - 1:
-            u_ref[...] = own
+            scale_ref[0] = own
 
         def columns(at):
             step = chips - at
-            col_send[k, step] = jnp.dot(
-                weights[...], cells[step], preferred_element_type=jnp.float32
-            )
+            sums = jnp.dot(weights[...], cells[step], preferred_element_type=jnp.float32)
+            if k == 0:
+                first_send[step] = sums
+            else:
+                before = first_send[step] if k == 1 else known[step]
+                change = (sums - before).astype(jnp.bfloat16)
+                col_send[k - 1, step] = change
+                if k < ITERS - 1:
+                    known[step] = before + change.astype(jnp.float32)
             col_copy(k, step).start()
 
         each(1, chips, columns)
-        total = jnp.dot(weights[...], cells[0], preferred_element_type=jnp.float32)
+        own_sums = jnp.dot(weights[...], cells[0], preferred_element_type=jnp.float32)
 
         def add_columns(step, total):
             col_copy(k, step).wait_recv()
-            return total + col_recv[k, step].astype(jnp.float32)
-
-        total = lax.fori_loop(1, chips, add_columns, total)
-        scale_v = observed_ref[...] / total
+            if k == 0:
+                return total + first_recv[step]
+            return total + col_recv[k - 1, step].astype(jnp.float32)
+
+        others = lax.fori_loop(1, chips, add_columns, others)
+        scale_v = observed_ref[...] / (own_sums + others)
         if k < ITERS - 1:
             v_send[k] = scale_v.astype(jnp.bfloat16)
             v_recv[k, 0] = scale_v.astype(jnp.bfloat16)
         else:
-            v_ref[...] = scale_v
+            scale_ref[1] = scale_v
 
     pred_copy.wait_send()
     predicted_copy.wait_send()
@@ -204,12 +230,15 @@
     vmem = pl.BlockSpec(memory_space=pltpu.VMEM)
     cell_bytes = chips * 2 * points * points * 2
     pairs = chips * 2 * points * points
-    scale_u, scale_v = pl.pallas_call(
+    scales = pl.pallas_call(
         functools.partial(kernel, chips),
-        out_shape=[jax.ShapeDtypeStruct((freqs, points), f32)] * 2,
-        in_specs=[vmem] * 4,
-        out_specs=[vmem] * 2,
+        out_shape=jax.ShapeDtypeStruct((2, freqs, points), f32),
+        in_specs=[pl.BlockSpec(memory_space=pltpu.HBM)] * 4,
+        out_specs=vmem,
         scratch_shapes=[
+            pltpu.VMEM((coords, points), f32),
+            pltpu.VMEM((freqs, points), f32),
+            pltpu.VMEM((freqs, points), f32),
             pltpu.VMEM((chips, coords, points), f32),
             pltpu.VMEM((coords, points), f32),
             pltpu.VMEM((freqs, points), f32),
@@ -217,12 +246,16 @@
             pltpu.VMEM((chips, 2 * points, points), bf16),
             pltpu.VMEM((2 * points, 128), f32),
             pltpu.VMEM((freqs, 2 * points), bf16),
-            pltpu.VMEM((ITERS, chips, freqs, points), f32),
-            pltpu.VMEM((ITERS, chips, freqs, points), f32),
+            pltpu.VMEM((chips, freqs, points), f32),
+            pltpu.VMEM((chips, freqs, points), f32),
+            pltpu.VMEM((ITERS - 1, chips, freqs, points), bf16),
+            pltpu.VMEM((ITERS - 1, chips, freqs, points), bf16),
+            pltpu.VMEM((chips, freqs, points), f32),
             pltpu.VMEM((ITERS - 1, freqs, points), bf16),
             pltpu.VMEM((ITERS - 1, chips, freqs, points), bf16),
             pltpu.VMEM((ITERS, freqs, 2 * points), f32),
             pltpu.VMEM((ITERS, freqs, 2 * points), f32),
+            pltpu.SemaphoreType.DMA((4,)),
             pltpu.SemaphoreType.DMA((2, chips)),
             pltpu.SemaphoreType.DMA((2, ITERS, chips)),
             pltpu.SemaphoreType.DMA((2, ITERS - 1, chips)),
@@ -238,7 +271,7 @@
             transcendentals=pairs,
         ),
     )(pred_points, obs_points, predicted, observed)
-    return jnp.log(scale_u), jnp.log(scale_v)
+    return jnp.log(scales[0]), jnp.log(scales[1])
 
 
 def solution(mesh):

time: 57.4 us -> 52.8 us (0.920)
  Pallas kernels: 52.2 us -> 48.2 us
  local copies, waits for them, and re-layouts: 4.19 us -> 3.58 us
    pallas_call x1, Pallas kernels: 52.2 us -> 48.2 us  [on_device(): pl.pallas_call(functools.partial(kernel, chips), out_shape=jax.ShapeDtype...]
    log x2 -> x1, local copies, waits for them, and re-layouts: 1.25 us -> 0.64 us  [on_device(): return (jnp.log(scales[0]), jnp.log(scales[1]))]
where the time goes in v2:
time: 52.8 us; the launch traced here: 52.5 us
  Pallas kernels  48.2 us (91%)
  local copies, waits for them, and re-layouts  3.58 us (7%)
  between operations  0.65 us (1%)
    pallas_call x1, Pallas kernels, on_device(): pl.pallas_call(functools.partial(kernel, chips), out_shape=jax.ShapeDtype...  48.2 us
    unnamed x8, local copies, waits for them, and re-layouts  2.94 us

profile of v2, /device:TPU:0, one launch (start us, length us, event | category | flops | bytes accessed | tf_op | source)
XLA Modules:
  0.0 52.5 jit_solution(1308584727316263532)
XLA Ops:
  0.6 0.0 copy-start
  0.6 0.7 %copy-done = f32[16,512]{1,0:T(8,128)S(1)} copy-done((f32[16,512]{1,0:T(8,128)S(1)}, f32[16,512]{1,0:T(8,128)}, u32[]{:S(2)}) %copy-start) | copy-done | bytes 32792
  1.4 0.0 copy-start.1
  1.4 0.8 %copy-done.1 = f32[16,512]{1,0:T(8,128)S(1)} copy-done((f32[16,512]{1,0:T(8,128)S(1)}, f32[16,512]{1,0:T(8,128)}, u32[]{:S(2)}) %copy-start.1) | copy-done | bytes 32792
  2.1 0.0 copy-start.2
  2.1 0.7 %copy-done.2 = f32[8,512]{1,0:T(8,128)S(1)} copy-done((f32[8,512]{1,0:T(8,128)S(1)}, f32[8,512]{1,0:T(8,128)}, u32[]{:S(2)}) %copy-start.2) | copy-done | bytes 16408
  2.9 0.0 copy-start.3
  2.9 0.7 %copy-done.3 = f32[8,512]{1,0:T(8,128)S(1)} copy-done((f32[8,512]{1,0:T(8,128)S(1)}, f32[8,512]{1,0:T(8,128)}, u32[]{:S(2)}) %copy-start.3) | copy-done | bytes 16408
  3.6 48.2 %shard_map.59 = f32[2,16,512]{2,1,0:T(8,128)S(1)} custom-call(f32[8,512]{1,0:T(8,128)S(1)} %copy-done.2, f32[8,512]{1,0:T(8,128)S(1)} %copy-done.3, f32[16,512]{1,0:T(8,128)S(1)} %copy-done, f32[16,512]{1,0:T(8,128)S(1)} %copy-done.1), custom_call_target="tpu_custom_call" | custom-call | flops 1207959552 | bytes 163840 | tf_op jit(solution)/shard_map/pallas_call | solution.py:233
  51.8 0.6 %log_bitcast_fusion = (f32[16,512]{1,0:T(8,128)}, f32[16,512]{1,0:T(8,128)}) fusion(f32[2,16,512]{2,1,0:T(8,128)S(1)} %shard_map.59), kind=kLoop, calls=%fused_computation | loop fusion | bytes 131072 | tf_op jit(solution)/shard_map/log | solution.py:274
Async XLA Ops:
  0.6 0.8 %copy-start = (f32[16,512]{1,0:T(8,128)S(1)}, f32[16,512]{1,0:T(8,128)}, u32[]{:S(2)}) copy-start(f32[16,512]{1,0:T(8,128)} %predicted_in.1) | copy-start | bytes 98308
  1.4 0.8 %copy-start.1 = (f32[16,512]{1,0:T(8,128)S(1)}, f32[16,512]{1,0:T(8,128)}, u32[]{:S(2)}) copy-start(f32[16,512]{1,0:T(8,128)} %observed_in.1) | copy-start | bytes 98308
  2.1 0.7 %copy-start.2 = (f32[8,512]{1,0:T(8,128)S(1)}, f32[8,512]{1,0:T(8,128)}, u32[]{:S(2)}) copy-start(f32[8,512]{1,0:T(8,128)} %pred_in.1) | copy-start | bytes 49156
  2.9 0.7 %copy-start.3 = (f32[8,512]{1,0:T(8,128)S(1)}, f32[8,512]{1,0:T(8,128)}, u32[]{:S(2)}) copy-start(f32[8,512]{1,0:T(8,128)} %obs_in.1) | copy-start | bytes 49156

commit v3 on v2

--- a/solution.py
+++ b/solution.py
@@ -134,7 +134,7 @@
     pl.semaphore_wait(barrier, chips)
 
     pred_copy.start()
-    each(1, chips, lambda at: obs_copy(chips - at).start())
+    each(1, chips, lambda step: obs_copy(step).start())
     fetches[2].wait()
     predicted_copy.start()
     fetches[3].wait()
@@ -155,7 +155,7 @@
     others = jnp.zeros((freqs, points), jnp.float32)
     for k in range(ITERS):
         if k > 0:
-            each(1, chips, lambda at: v_copy(k - 1, chips - at).start())
+            each(1, chips, lambda step: v_copy(k - 1, step).start())
 
             def add_rows(step, total):
                 @pl.when(step > 0)
@@ -228,7 +228,6 @@
     freqs = predicted.shape[0]
     f32, bf16 = jnp.float32, jnp.bfloat16
     vmem = pl.BlockSpec(memory_space=pltpu.VMEM)
-    cell_bytes = chips * 2 * points * points * 2
     pairs = chips * 2 * points * points
     scales = pl.pallas_call(
         functools.partial(kernel, chips),
@@ -263,7 +262,7 @@
         ],
         compiler_params=pltpu.CompilerParams(
             collective_id=0, has_side_effects=True,
-            vmem_limit_bytes=cell_bytes + 24 * 2**20,
+            vmem_limit_bytes=64 * 2**20,
         ),
         cost_estimate=pl.CostEstimate(
             flops=pairs * (2 * DEPTH + 5 * 2 * freqs),

time: 52.8 us -> 50 us (0.947)
  local copies, waits for them, and re-layouts: 3.58 us -> 1.41 us
    unnamed x8 -> x0, local copies, waits for them, and re-layouts: 2.94 us -> none
    log x1, local copies, waits for them, and re-layouts: 0.64 us -> 1.41 us  [on_device(): return (jnp.log(scales[0]), jnp.log(scales[1]))]
    pallas_call x1, Pallas kernels: 48.2 us -> 47.7 us  [on_device(): pl.pallas_call(functools.partial(kernel, chips), out_shape=jax.ShapeDtype...]
where the time goes in v3:
time: 50 us; the launch traced here: 49.7 us
  Pallas kernels  47.7 us (95%)
  local copies, waits for them, and re-layouts  1.41 us (3%)
  between operations  0.64 us (1%)
    pallas_call x1, Pallas kernels, on_device(): pl.pallas_call(functools.partial(kernel, chips), out_shape=jax.ShapeDtype...  47.7 us
    log x1, local copies, waits for them, and re-layouts, on_device(): return (jnp.log(scales[0]), jnp.log(scales[1]))  1.41 us

profile of v3, /device:TPU:0, one launch (start us, length us, event | category | flops | bytes accessed | tf_op | source)
XLA Modules:
  0.0 49.7 jit_solution(9949192507888072219)
XLA Ops:
  0.6 47.7 %shard_map.59 = f32[2,16,512]{2,1,0:T(8,128)} custom-call(f32[8,512]{1,0:T(8,128)} %pred_in.1, f32[8,512]{1,0:T(8,128)} %obs_in.1, f32[16,512]{1,0:T(8,128)} %predicted_in.1, f32[16,512]{1,0:T(8,128)} %observed_in.1), custom_call_target="tpu_custom_call" | custom-call | flops 1207959552 | bytes 163840 | tf_op jit(solution)/shard_map/pallas_call | solution.py:232
  48.3 1.4 %log_bitcast_fusion = (f32[16,512]{1,0:T(8,128)}, f32[16,512]{1,0:T(8,128)}) fusion(f32[2,16,512]{2,1,0:T(8,128)} %shard_map.59), kind=kLoop, calls=%fused_computation | loop fusion | bytes 131072 | tf_op jit(solution)/shard_map/log | solution.py:273

commit v4 on v3

--- a/solution.py
+++ b/solution.py
@@ -10,14 +10,6 @@
 ITERS = 3
 ENTROPY = 0.1
 DEPTH = 64
-
-
-def xor_index(left, right, bits):
-    total = 0
-    for bit in range(bits):
-        unit = 1 << bit
-        total = total + unit * ((left // unit + right // unit) % 2)
-    return total
 
 
 def three_parts(value):
@@ -50,7 +42,7 @@
 def kernel(
     chips, pred_in, obs_in, predicted_in, observed_in, scale_ref,
     pred_ref, predicted_ref, observed_ref,
-    obs_buf, pred_buf, predicted_buf, source, cells, acc, weights,
+    obs_buf, pred_buf, predicted_buf, source, source_t, cells, cells_t, acc, weights,
     first_send, first_recv, col_send, col_recv, known,
     v_send, v_recv, row_send, row_recv,
     in_sems, obs_sems, col_sems, v_sems, sib_sems,
@@ -62,14 +54,22 @@
     sibling = {"row": me + 1 - 2 * core}
     bits = chips.bit_length() - 1
     power = chips == 1 << bits
+    flips = [(1 << bit) * (1 - 2 * ((chip // (1 << bit)) % 2)) for bit in range(bits)]
+
+    def partner(step, forward):
+        if not isinstance(step, int):
+            return sibling
+        if power:
+            other = chip + sum(flips[bit] for bit in range(bits) if step >> bit & 1)
+        else:
+            other = (chip + (step if forward else chips - step)) % chips
+        return {"row": other * 2 + core}
 
     def ahead(step):
-        other = xor_index(chip, step, bits) if power else (chip + step) % chips
-        return {"row": other * 2 + core}
+        return partner(step, True)
 
     def behind(step):
-        other = xor_index(chip, step, bits) if power else (chip + chips - step) % chips
-        return {"row": other * 2 + core}
+        return partner(step, False)
 
     def remote(src, dst, sems, place, target):
         return pltpu.make_async_remote_copy(
@@ -109,8 +109,9 @@
         fetch.start()
     barrier = pltpu.get_barrier_semaphore()
     pl.semaphore_signal(barrier, inc=1, device_id=sibling, device_id_type=pl.DeviceIdType.MESH)
-    each(1, chips, lambda step: pl.semaphore_signal(
-        barrier, inc=1, device_id=ahead(step), device_id_type=pl.DeviceIdType.MESH))
+    for step in range(1, chips):
+        pl.semaphore_signal(
+            barrier, inc=1, device_id=ahead(step), device_id_type=pl.DeviceIdType.MESH)
     acc[...] = jnp.zeros_like(acc)
     tile = min(256, points)
 
@@ -127,19 +128,24 @@
             acc[rows] = sums
 
     fetches[0].wait()
-    source[:points] = operand(pred_ref[...], True).T.astype(jnp.bfloat16)
+    pred_operand = operand(pred_ref[...], True)
+    source[:points] = pred_operand.T.astype(jnp.bfloat16)
+    source_t[:, :points] = pred_operand.astype(jnp.bfloat16)
     fetches[1].wait()
     own_target = operand(obs_buf[0], False).astype(jnp.bfloat16)
     build(0, own_target, 0, points)
     pl.semaphore_wait(barrier, chips)
 
     pred_copy.start()
-    each(1, chips, lambda step: obs_copy(step).start())
+    for step in range(1, chips):
+        obs_copy(step).start()
     fetches[2].wait()
     predicted_copy.start()
     fetches[3].wait()
     pred_copy.wait_recv()
-    source[points:] = operand(pred_buf[...], True).T.astype(jnp.bfloat16)
+    pred_operand = operand(pred_buf[...], True)
+    source[points:] = pred_operand.T.astype(jnp.bfloat16)
+    source_t[:, points:] = pred_operand.astype(jnp.bfloat16)
     build(0, own_target, points, 2 * points)
 
     def build_next(step):
@@ -147,6 +153,13 @@
         build(step, operand(obs_buf[step], False).astype(jnp.bfloat16), 0, 2 * points)
 
     each(1, chips, build_next)
+    def build_transposed(step):
+        target = operand(obs_buf[step], False).T.astype(jnp.bfloat16)
+        for first in range(0, points, tile):
+            exponent = jnp.dot(
+                target[first:first + tile], source_t[...], preferred_element_type=jnp.float32)
+            cells_t[step, first:first + tile] = jnp.exp(exponent).astype(jnp.bfloat16)
+
     row_sums = jnp.sum(acc[...].T, axis=0, keepdims=True)
     row_send[0] = jnp.broadcast_to(row_sums, row_send.shape[1:])
     row_copy(0).start()
@@ -155,17 +168,16 @@
     others = jnp.zeros((freqs, points), jnp.float32)
     for k in range(ITERS):
         if k > 0:
-            each(1, chips, lambda step: v_copy(k - 1, step).start())
+            for step in range(1, chips):
+                v_copy(k - 1, step).start()
 
             def add_rows(step, total):
                 @pl.when(step > 0)
                 def _():
                     v_copy(k - 1, step).wait_recv()
 
-                return total + lax.dot_general(
-                    v_recv[k - 1, step], cells[step], (((1,), (1,)), ((), ())),
-                    preferred_element_type=jnp.float32,
-                )
+                return total + jnp.dot(
+                    v_recv[k - 1, step], cells_t[step], preferred_element_type=jnp.float32)
 
             row_send[k] = lax.fori_loop(
                 0, chips, add_rows, jnp.zeros((freqs, 2 * points), jnp.float32))
@@ -178,8 +190,7 @@
         if k == ITERS - 1:
             scale_ref[0] = own
 
-        def columns(at):
-            step = chips - at
+        def columns(step):
             sums = jnp.dot(weights[...], cells[step], preferred_element_type=jnp.float32)
             if k == 0:
                 first_send[step] = sums
@@ -191,8 +202,12 @@
                     known[step] = before + change.astype(jnp.float32)
             col_copy(k, step).start()
 
-        each(1, chips, columns)
+        for step in range(chips - 1, 0, -1):
+            columns(step)
         own_sums = jnp.dot(weights[...], cells[0], preferred_element_type=jnp.float32)
+
+        if k == 0:
+            each(0, chips, build_transposed)
 
         def add_columns(step, total):
             col_copy(k, step).wait_recv()
@@ -242,7 +257,9 @@
             pltpu.VMEM((coords, points), f32),
             pltpu.VMEM((freqs, points), f32),
             pltpu.VMEM((2 * points, DEPTH), bf16),
+            pltpu.VMEM((DEPTH, 2 * points), bf16),
             pltpu.VMEM((chips, 2 * points, points), bf16),
+            pltpu.VMEM((chips, points, 2 * points), bf16),
             pltpu.VMEM((2 * points, 128), f32),
             pltpu.VMEM((freqs, 2 * points), bf16),
             pltpu.VMEM((chips, freqs, points), f32),
@@ -265,9 +282,9 @@
             vmem_limit_bytes=64 * 2**20,
         ),
         cost_estimate=pl.CostEstimate(
-            flops=pairs * (2 * DEPTH + 5 * 2 * freqs),
+            flops=pairs * (4 * DEPTH + 5 * 2 * freqs),
             bytes_accessed=4 * points * (2 * coords + 4 * freqs),
-            transcendentals=pairs,
+            transcendentals=2 * pairs,
         ),
     )(pred_points, obs_points, predicted, observed)
     return jnp.log(scales[0]), jnp.log(scales[1])

time: 50 us -> 48.6 us (0.972)
  Pallas kernels: 47.7 us -> 45.9 us
    pallas_call x1, Pallas kernels: 47.7 us -> 45.9 us  [on_device(): pl.pallas_call(functools.partial(kernel, chips), out_shape=jax.ShapeDtype...]
where the time goes in v4:
time: 48.6 us; the launch traced here: 48 us
  Pallas kernels  45.9 us (94%)
  local copies, waits for them, and re-layouts  1.41 us (3%)
  between operations  0.64 us (1%)
    pallas_call x1, Pallas kernels, on_device(): pl.pallas_call(functools.partial(kernel, chips), out_shape=jax.ShapeDtype...  45.9 us
    log x1, local copies, waits for them, and re-layouts, on_device(): return (jnp.log(scales[0]), jnp.log(scales[1]))  1.41 us

profile of v4, /device:TPU:0, one launch (start us, length us, event | category | flops | bytes accessed | tf_op | source)
XLA Modules:
  0.0 48.0 jit_solution(7653332110717244891)
XLA Ops:
  0.6 45.9 %shard_map.59 = f32[2,16,512]{2,1,0:T(8,128)} custom-call(f32[8,512]{1,0:T(8,128)} %pred_in.1, f32[8,512]{1,0:T(8,128)} %obs_in.1, f32[16,512]{1,0:T(8,128)} %predicted_in.1, f32[16,512]{1,0:T(8,128)} %observed_in.1), custom_call_target="tpu_custom_call" | custom-call | flops 1744830464 | bytes 163840 | tf_op jit(solution)/shard_map/pallas_call | solution.py:247
  46.6 1.4 %log_bitcast_fusion = (f32[16,512]{1,0:T(8,128)}, f32[16,512]{1,0:T(8,128)}) fusion(f32[2,16,512]{2,1,0:T(8,128)} %shard_map.59), kind=kLoop, calls=%fused_computation | loop fusion | bytes 131072 | tf_op jit(solution)/shard_map/log | solution.py:290

commit v5 on v4

--- a/solution.py
+++ b/solution.py
@@ -133,7 +133,6 @@
     source_t[:, :points] = pred_operand.astype(jnp.bfloat16)
     fetches[1].wait()
     own_target = operand(obs_buf[0], False).astype(jnp.bfloat16)
-    build(0, own_target, 0, points)
     pl.semaphore_wait(barrier, chips)
 
     pred_copy.start()
@@ -142,6 +141,7 @@
     fetches[2].wait()
     predicted_copy.start()
     fetches[3].wait()
+    build(0, own_target, 0, points)
     pred_copy.wait_recv()
     pred_operand = operand(pred_buf[...], True)
     source[points:] = pred_operand.T.astype(jnp.bfloat16)
@@ -168,19 +168,19 @@
     others = jnp.zeros((freqs, points), jnp.float32)
     for k in range(ITERS):
         if k > 0:
-            for step in range(1, chips):
+            for step in range(chips - 1, 0, -1):
                 v_copy(k - 1, step).start()
 
             def add_rows(step, total):
-                @pl.when(step > 0)
-                def _():
+                if step > 0:
                     v_copy(k - 1, step).wait_recv()
-
                 return total + jnp.dot(
                     v_recv[k - 1, step], cells_t[step], preferred_element_type=jnp.float32)
 
-            row_send[k] = lax.fori_loop(
-                0, chips, add_rows, jnp.zeros((freqs, 2 * points), jnp.float32))
+            products = jnp.zeros((freqs, 2 * points), jnp.float32)
+            for step in range(chips):
+                products = add_rows(step, products)
+            row_send[k] = products
             row_copy(k).start()
         row_copy(k).wait_recv()
         own = predicted_ref[...] / (row_send[k, :, :points] + row_recv[k, :, points:])
@@ -215,7 +215,8 @@
                 return total + first_recv[step]
             return total + col_recv[k - 1, step].astype(jnp.float32)
 
-        others = lax.fori_loop(1, chips, add_columns, others)
+        for step in range(1, chips):
+            others = add_columns(step, others)
         scale_v = observed_ref[...] / (own_sums + others)
         if k < ITERS - 1:
             v_send[k] = scale_v.astype(jnp.bfloat16)

time: 48.6 us -> 48.3 us (level)
  no operation moved by 1% of the time
where the time goes in v5:
time: 48.3 us; the launch traced here: 48 us
  Pallas kernels  46 us (95%)
  local copies, waits for them, and re-layouts  1.41 us (3%)
  between operations  0.64 us (1%)
    pallas_call x1, Pallas kernels, on_device(): pl.pallas_call(functools.partial(kernel, chips), out_shape=jax.ShapeDtype...  46 us
    log x1, local copies, waits for them, and re-layouts, on_device(): return (jnp.log(scales[0]), jnp.log(scales[1]))  1.41 us

profile of v5, /device:TPU:0, one launch (start us, length us, event | category | flops | bytes accessed | tf_op | source)
XLA Modules:
  0.0 48.0 jit_solution(8260569001386807042)
XLA Ops:
  0.6 46.0 %shard_map.59 = f32[2,16,512]{2,1,0:T(8,128)} custom-call(f32[8,512]{1,0:T(8,128)} %pred_in.1, f32[8,512]{1,0:T(8,128)} %obs_in.1, f32[16,512]{1,0:T(8,128)} %predicted_in.1, f32[16,512]{1,0:T(8,128)} %observed_in.1), custom_call_target="tpu_custom_call" | custom-call | flops 1744830464 | bytes 163840 | tf_op jit(solution)/shard_map/pallas_call | solution.py:248
  46.6 1.4 %log_bitcast_fusion = (f32[16,512]{1,0:T(8,128)}, f32[16,512]{1,0:T(8,128)}) fusion(f32[2,16,512]{2,1,0:T(8,128)} %shard_map.59), kind=kLoop, calls=%fused_computation | loop fusion | bytes 131072 | tf_op jit(solution)/shard_map/log | solution.py:291
